TPU v7x, 32 devices: a whole 2x2x4 slice. The times are simulated.
32 devices in a mesh: dp: 2 (over x), outer: 8 (over z, core), inner: 2 (over y).
Axes of the slice: x: 2, y: 2, z: 4, core: 2. Of those that a mesh axis runs over, the one named last changes fastest.
Arguments:
- queries: bfloat16 [2048, 4096], P(('outer', 'inner'), 'dp'), may hold values from -512 to 512
- out_grad: bfloat16 [2048, 4096], P(('outer', 'inner'), 'dp'), may hold values from -6 to 6
- key_rows: bfloat16 [2048, 512], P(('outer', 'inner')), may hold values from -14 to 14
- value_rows: bfloat16 [2048, 512], P(('outer', 'inner')), may hold values from -6 to 6
- block_order: int32 [16], replicated, may hold values from 0 to 15, each once
- block_flags: int32 [16, 3], replicated, may hold values 0 or 1
Outputs:
- query_grad: bfloat16 [2048, 4096], P(('outer', 'inner'), 'dp')
- key_grad: float32 [2048, 512], P(('outer', 'inner'), 'dp')
- value_grad: float32 [2048, 512], P(('outer', 'inner'), 'dp')
Inputs may be any that keep to these rules, and one draw needn't show every extreme that they name: `block_order`: each number appears once.
All inputs are finite; a program needn't handle non-finite values.
Results may differ from a plain program's by a relative error of at most 0.005.
Values may be sent and summed in bfloat16 or wider, within the bound.
A program may use at most 64 MiB of HBM per device.

v0:
```python
import math

import jax
import jax.numpy as jnp
from jax import lax
from jax.sharding import PartitionSpec as P

HD = 128


def passed_along(x, axis, by):
    devices = lax.axis_size(axis)
    return lax.ppermute(x, axis, [(i, (i + by) % devices) for i in range(devices)])


def body(queries, out_grad, key_rows, value_rows, block_order, block_flags):
    row_count = queries.shape[0]
    key_heads = key_rows.shape[1] // HD
    local_groups = queries.shape[1] // (key_heads * HD)
    inner_size = lax.axis_size("inner")
    outer_size = lax.axis_size("outer")
    outer_index = lax.axis_index("outer")
    member_index = lax.axis_index("inner")
    shard_index = outer_index * inner_size + member_index
    previous = (outer_index + outer_size - 1) % outer_size * inner_size + member_index
    group_keys, group_values = (
        lax.all_gather(key_rows, "inner", axis=0, tiled=True),
        lax.all_gather(value_rows, "inner", axis=0, tiled=True),
    )
    prev_keys, prev_values = passed_along((key_rows, value_rows), "outer", 1)
    group_span = inner_size * row_count
    key_window = jnp.concatenate([group_keys, prev_keys], 0).reshape(
        group_span + row_count, key_heads, HD
    )
    value_window = jnp.concatenate([group_values, prev_values], 0).reshape(
        group_span + row_count, key_heads, HD
    )
    row_index = jnp.arange(row_count, dtype=jnp.int32)
    group_blocks = lax.dynamic_slice_in_dim(block_order, outer_index * inner_size, inner_size, 0)
    prev_block = lax.dynamic_slice_in_dim(block_order, previous, 1, 0)
    own_block = lax.dynamic_slice_in_dim(block_order, shard_index, 1, 0)
    key_pos = (
        jnp.concatenate([group_blocks, prev_block], 0)[:, None] * row_count + row_index[None, :]
    ).reshape(-1)
    query_pos = own_block * row_count + row_index
    flag_row = lax.dynamic_slice(block_flags, (shard_index, 0), (1, inner_size + 1))[0]
    allowed = (flag_row == 1) | (jnp.arange(inner_size + 1, dtype=jnp.int32) == member_index)
    visible = (key_pos[None, :] <= query_pos[:, None]) & jnp.repeat(allowed, row_count)[None, :]
    seen = visible[None]
    score_scale = 1.0 / math.sqrt(HD)
    query_stack = queries.reshape(row_count, local_groups, key_heads, HD).transpose(1, 0, 2, 3)
    grad_stack = out_grad.reshape(row_count, local_groups, key_heads, HD).transpose(1, 0, 2, 3)

    def head_group(totals, blocks_in):
        key_sum, value_sum = totals
        query_block, grad_block = blocks_in
        scores = (
            jnp.einsum("rjd,wjd->jrw", query_block, key_window, preferred_element_type=jnp.float32)
            * score_scale
        )
        row_max = jnp.max(jnp.where(seen, scores, -jnp.inf), axis=-1, keepdims=True)
        exp_scores = jnp.where(seen, jnp.exp(scores - row_max), 0.0)
        soft_weights = exp_scores / jnp.sum(exp_scores, axis=-1, keepdims=True)
        soft_low = soft_weights.astype(jnp.bfloat16)
        weight_grads = jnp.einsum(
            "rjd,wjd->jrw", grad_block, value_window, preferred_element_type=jnp.float32
        )
        row_delta = jnp.sum(soft_weights * weight_grads, axis=-1, keepdims=True)
        score_grads = (soft_weights * (weight_grads - row_delta) * score_scale).astype(jnp.bfloat16)
        query_part = jnp.einsum(
            "jrw,wjd->rjd", score_grads, key_window, preferred_element_type=jnp.float32
        ).astype(jnp.bfloat16)
        key_sum = key_sum + jnp.einsum(
            "jrw,rjd->wjd", score_grads, query_block, preferred_element_type=jnp.float32
        )
        value_sum = value_sum + jnp.einsum(
            "jrw,rjd->wjd", soft_low, grad_block, preferred_element_type=jnp.float32
        )
        return ((key_sum, value_sum), query_part)

    zero_sums = jnp.zeros((group_span + row_count, key_heads, HD), jnp.float32)
    (key_sum, value_sum), query_parts = lax.scan(
        head_group, (zero_sums, zero_sums), (query_stack, grad_stack)
    )
    query_grad = query_parts.transpose(1, 0, 2, 3).reshape(row_count, local_groups * key_heads * HD)
    back_keys, back_values = (
        passed_along(key_sum[group_span:].astype(jnp.bfloat16), "outer", -1).astype(jnp.float32),
        passed_along(value_sum[group_span:].astype(jnp.bfloat16), "outer", -1).astype(jnp.float32),
    )
    own_keys, own_values = (
        lax.psum_scatter(key_sum[:group_span], "inner", scatter_dimension=0, tiled=True),
        lax.psum_scatter(value_sum[:group_span], "inner", scatter_dimension=0, tiled=True),
    )
    key_grad, value_grad = (
        lax.psum_scatter(own_keys + back_keys, "dp", scatter_dimension=1, tiled=True),
        lax.psum_scatter(own_values + back_values, "dp", scatter_dimension=1, tiled=True),
    )
    return (query_grad, key_grad.reshape(row_count, -1), value_grad.reshape(row_count, -1))


def solution(mesh):
    placed = (
        P(("outer", "inner"), "dp"),
        P(("outer", "inner"), "dp"),
        P(("outer", "inner"), None),
        P(("outer", "inner"), None),
        P(),
        P(),
    )
    return jax.shard_map(
        body,
        mesh=mesh,
        in_specs=placed,
        out_specs=(
            P(("outer", "inner"), "dp"),
            P(("outer", "inner"), "dp"),
            P(("outer", "inner"), "dp"),
        ),
        check_vma=False,
    )
```

profile of v0, /device:TPU:0, one launch (start us, length us, event | category | flops | bytes accessed | tf_op | source)
XLA Modules:
  0.0 154.0 jit_solution(11857496296782894228)
XLA Ops:
  8.9 2.7 %collective-permute-start.1 = (bf16[128,512]{0,1:T(8,128)(2,1)S(1)}, bf16[128,512]{0,1:T(8,128)(2,1)S(1)}, u32[]{:S(2)}, u32[]{:S(2)}) collective-permute-start(bf16[128,512]{0,1:T(8,128)(2,1)S(1)} %copy.20), channel_id=1, source_target_pairs={{0,2},{2,4},{4,6},{6,8},{8,10},{10,12},{12,14},{14,0},{1,3},{3,5},... | collective-permute-start | bytes 393224 | tf_op jit(solution)/shard_map/ppermute | solution.py:13
  14.1 6.1 %all_gather.6 = bf16[256,512]{0,1:T(8,128)(2,1)S(1)} all-gather(bf16[128,512]{0,1:T(8,128)(2,1)S(1)} %copy.17), channel_id=1, replica_groups=mesh['dp'=2,'outer'=8,'inner'=2] {'inner'}, dimensions={0}, use_global_device_ids=true | all-gather | bytes 393216 | tf_op jit(solution)/shard_map/all_gather | solution.py:27
  20.2 5.7 %all_gather.7 = bf16[256,512]{0,1:T(8,128)(2,1)S(1)} all-gather(bf16[128,512]{0,1:T(8,128)(2,1)S(1)} %copy.20), channel_id=1, replica_groups=mesh['dp'=2,'outer'=8,'inner'=2] {'inner'}, dimensions={0}, use_global_device_ids=true | all-gather | bytes 393216 | tf_op jit(solution)/shard_map/all_gather | solution.py:28
  28.5 55.6 %while.15 = (s32[]{:T(128)}, f32[384,4,128]{0,2,1:T(8,128)}, f32[384,4,128]{0,2,1:T(8,128)}, bf16[4,128,4,128]{3,1,2,0:T(8,128)(2,1)}, bf16[4,128,4,128]{1,3,2,0...) while((s32[]{:T(128)}, f32[384,4,128]{0,2,1:T(8,128)}, ...), condition=%wide.region_4.5_spmd.clone, body=%wide.region_0.4_spmd.clone.sunk | while | flops 257330176 | bytes 16204808 | solution.py:82
  28.5 1.2 convolution_multiply_fusion.2
  31.4 3.3 %fusion.84 = bf16[4,128,4,128]{3,1,2,0:T(8,128)(2,1)} fusion(bf16[4,128,4,128]{3,1,2,0:T(8,128)(2,1)} %get-tuple-element.220, s32[]{:T(128)} %get-tuple-element.217, bf16[384,4,128]{2,0,1:T(8,128)(2,1)S(1)} %get-tuple-element.235, f32[4,128,384]{2,1,0:T(8,128)S(1)} %fusion.80, f32[4,128,384]{2,1,0:T(8,128)S(1)} %get-tuple-element.202, ...), kind=kOutput, calls=%fused_computation.17.clone.1 | convolution fusion | flops 51774336 | bytes 3674624 | tf_op jit(solution)/shard_map/while/body/eval_jaxpr/jrw,wjd->rjd/dot_general | solution.py:70
  34.7 2.9 %fusion.83 = f32[384,4,128]{0,2,1:T(8,128)} fusion(f32[384,4,128]{0,2,1:T(8,128)} %get-tuple-element.219, pred[]{:T(512)S(6)} %compare.4, bf16[4,128,4,128]{1,3,2,0:T(8,128)(2,1)} %get-tuple-element.236, s32[]{:T(128)} %get-tuple-element.217, f32[4,128]{1,0:T(4,128)S(1)} %get-tuple-element.203, f32[4,128,384]{2,1,0:T(8,128)S(1)} %convolution_multiply_fusion.2, ...), kind=kOutput, calls=%fused_computation.10.clone.1 | convolution fusion | flops 51708800 | bytes 3377665 | tf_op jit(solution)/shard_map/while/body/eval_jaxpr/jrw,rjd->wjd/dot_general | solution.py:76
  37.6 4.4 %fusion.82 = f32[384,4,128]{0,2,1:T(8,128)} fusion(f32[4,128,384]{2,1,0:T(8,128)S(1)} %fusion.80, f32[384,4,128]{0,2,1:T(8,128)} %get-tuple-element.218, pred[]{:T(512)S(6)} %compare.4, bf16[4,128,4,128]{1,3,2,0:T(8,128)(2,1)} %get-tuple-element.234, s32[]{:T(128)} %get-tuple-element.217, f32[4,128,384]{2,1,0:T(8,128)S(1)} %get-tuple-element.202, ...), kind=kOutput, calls=%fused_computation.12.clone.1 | convolution fusion | flops 52102016 | bytes 4854273 | tf_op jit(solution)/shard_map/while/body/eval_jaxpr/jrw,rjd->wjd/dot_general | solution.py:73
  43.7 1.2 fusion.80
  44.9 3.3 %fusion.84 = bf16[4,128,4,128]{3,1,2,0:T(8,128)(2,1)} fusion(bf16[4,128,4,128]{3,1,2,0:T(8,128)(2,1)} %get-tuple-element.220, s32[]{:T(128)} %get-tuple-element.217, bf16[384,4,128]{2,0,1:T(8,128)(2,1)S(1)} %get-tuple-element.235, f32[4,128,384]{2,1,0:T(8,128)S(1)} %fusion.80, f32[4,128,384]{2,1,0:T(8,128)S(1)} %get-tuple-element.202, ...), kind=kOutput, calls=%fused_computation.17.clone.1 | convolution fusion | flops 51774336 | bytes 3674624 | tf_op jit(solution)/shard_map/while/body/eval_jaxpr/jrw,wjd->rjd/dot_general | solution.py:70
  48.1 3.2 %fusion.83 = f32[384,4,128]{0,2,1:T(8,128)} fusion(f32[384,4,128]{0,2,1:T(8,128)} %get-tuple-element.219, pred[]{:T(512)S(6)} %compare.4, bf16[4,128,4,128]{1,3,2,0:T(8,128)(2,1)} %get-tuple-element.236, s32[]{:T(128)} %get-tuple-element.217, f32[4,128]{1,0:T(4,128)S(1)} %get-tuple-element.203, f32[4,128,384]{2,1,0:T(8,128)S(1)} %convolution_multiply_fusion.2, ...), kind=kOutput, calls=%fused_computation.10.clone.1 | convolution fusion | flops 51708800 | bytes 3377665 | tf_op jit(solution)/shard_map/while/body/eval_jaxpr/jrw,rjd->wjd/dot_general | solution.py:76
  51.3 4.7 %fusion.82 = f32[384,4,128]{0,2,1:T(8,128)} fusion(f32[4,128,384]{2,1,0:T(8,128)S(1)} %fusion.80, f32[384,4,128]{0,2,1:T(8,128)} %get-tuple-element.218, pred[]{:T(512)S(6)} %compare.4, bf16[4,128,4,128]{1,3,2,0:T(8,128)(2,1)} %get-tuple-element.234, s32[]{:T(128)} %get-tuple-element.217, f32[4,128,384]{2,1,0:T(8,128)S(1)} %get-tuple-element.202, ...), kind=kOutput, calls=%fused_computation.12.clone.1 | convolution fusion | flops 52102016 | bytes 4854273 | tf_op jit(solution)/shard_map/while/body/eval_jaxpr/jrw,rjd->wjd/dot_general | solution.py:73
  57.7 1.2 fusion.80
  58.9 3.3 %fusion.84 = bf16[4,128,4,128]{3,1,2,0:T(8,128)(2,1)} fusion(bf16[4,128,4,128]{3,1,2,0:T(8,128)(2,1)} %get-tuple-element.220, s32[]{:T(128)} %get-tuple-element.217, bf16[384,4,128]{2,0,1:T(8,128)(2,1)S(1)} %get-tuple-element.235, f32[4,128,384]{2,1,0:T(8,128)S(1)} %fusion.80, f32[4,128,384]{2,1,0:T(8,128)S(1)} %get-tuple-element.202, ...), kind=kOutput, calls=%fused_computation.17.clone.1 | convolution fusion | flops 51774336 | bytes 3674624 | tf_op jit(solution)/shard_map/while/body/eval_jaxpr/jrw,wjd->rjd/dot_general | solution.py:70
  62.2 3.2 %fusion.83 = f32[384,4,128]{0,2,1:T(8,128)} fusion(f32[384,4,128]{0,2,1:T(8,128)} %get-tuple-element.219, pred[]{:T(512)S(6)} %compare.4, bf16[4,128,4,128]{1,3,2,0:T(8,128)(2,1)} %get-tuple-element.236, s32[]{:T(128)} %get-tuple-element.217, f32[4,128]{1,0:T(4,128)S(1)} %get-tuple-element.203, f32[4,128,384]{2,1,0:T(8,128)S(1)} %convolution_multiply_fusion.2, ...), kind=kOutput, calls=%fused_computation.10.clone.1 | convolution fusion | flops 51708800 | bytes 3377665 | tf_op jit(solution)/shard_map/while/body/eval_jaxpr/jrw,rjd->wjd/dot_general | solution.py:76
  65.4 4.7 %fusion.82 = f32[384,4,128]{0,2,1:T(8,128)} fusion(f32[4,128,384]{2,1,0:T(8,128)S(1)} %fusion.80, f32[384,4,128]{0,2,1:T(8,128)} %get-tuple-element.218, pred[]{:T(512)S(6)} %compare.4, bf16[4,128,4,128]{1,3,2,0:T(8,128)(2,1)} %get-tuple-element.234, s32[]{:T(128)} %get-tuple-element.217, f32[4,128,384]{2,1,0:T(8,128)S(1)} %get-tuple-element.202, ...), kind=kOutput, calls=%fused_computation.12.clone.1 | convolution fusion | flops 52102016 | bytes 4854273 | tf_op jit(solution)/shard_map/while/body/eval_jaxpr/jrw,rjd->wjd/dot_general | solution.py:73
  71.8 1.2 fusion.80
  73.0 3.3 %fusion.84 = bf16[4,128,4,128]{3,1,2,0:T(8,128)(2,1)} fusion(bf16[4,128,4,128]{3,1,2,0:T(8,128)(2,1)} %get-tuple-element.220, s32[]{:T(128)} %get-tuple-element.217, bf16[384,4,128]{2,0,1:T(8,128)(2,1)S(1)} %get-tuple-element.235, f32[4,128,384]{2,1,0:T(8,128)S(1)} %fusion.80, f32[4,128,384]{2,1,0:T(8,128)S(1)} %get-tuple-element.202, ...), kind=kOutput, calls=%fused_computation.17.clone.1 | convolution fusion | flops 51774336 | bytes 3674624 | tf_op jit(solution)/shard_map/while/body/eval_jaxpr/jrw,wjd->rjd/dot_general | solution.py:70
  76.3 3.2 %fusion.83 = f32[384,4,128]{0,2,1:T(8,128)} fusion(f32[384,4,128]{0,2,1:T(8,128)} %get-tuple-element.219, pred[]{:T(512)S(6)} %compare.4, bf16[4,128,4,128]{1,3,2,0:T(8,128)(2,1)} %get-tuple-element.236, s32[]{:T(128)} %get-tuple-element.217, f32[4,128]{1,0:T(4,128)S(1)} %get-tuple-element.203, f32[4,128,384]{2,1,0:T(8,128)S(1)} %convolution_multiply_fusion.2, ...), kind=kOutput, calls=%fused_computation.10.clone.1 | convolution fusion | flops 51708800 | bytes 3377665 | tf_op jit(solution)/shard_map/while/body/eval_jaxpr/jrw,rjd->wjd/dot_general | solution.py:76
  79.4 4.7 %fusion.82 = f32[384,4,128]{0,2,1:T(8,128)} fusion(f32[4,128,384]{2,1,0:T(8,128)S(1)} %fusion.80, f32[384,4,128]{0,2,1:T(8,128)} %get-tuple-element.218, pred[]{:T(512)S(6)} %compare.4, bf16[4,128,4,128]{1,3,2,0:T(8,128)(2,1)} %get-tuple-element.234, s32[]{:T(128)} %get-tuple-element.217, f32[4,128,384]{2,1,0:T(8,128)S(1)} %get-tuple-element.202, ...), kind=kOutput, calls=%fused_computation.12.clone.1 | convolution fusion | flops 52102016 | bytes 4854273 | tf_op jit(solution)/shard_map/while/body/eval_jaxpr/jrw,rjd->wjd/dot_general | solution.py:73
  84.1 2.0 %slice.16 = f32[256,4,128]{0,2,1:T(8,128)} slice(f32[384,4,128]{0,2,1:T(8,128)} %get-tuple-element.54), slice={[0:256], [0:4], [0:128]} | slice | bytes 1048576 | tf_op jit(solution)/shard_map/slice | solution.py:92
  88.1 2.5 %collective-permute-done.3 = bf16[128,4,128]{0,2,1:T(8,128)(2,1)S(1)} collective-permute-done((bf16[128,4,128]{0,2,1:T(8,128)(2,1)S(1)}, bf16[128,4,128]{0,2,1:T(8,128)(2,1)S(1)}, u32[]{:S(2)}, u32[]{:S(2)}) %collective-permute-start.3) | collective-permute-done | bytes 131104 | tf_op jit(solution)/shard_map/ppermute | solution.py:13
  90.7 10.4 %reduce-scatter.9.cloned.1.call-done = f32[128,4,128]{0,2,1:T(8,128)} async-done(((f32[256,4,128]{0,2,1:T(8,128)}), f32[128,4,128]{0,2,1:T(8,128)}) %reduce-scatter.9.cloned.1.call-update) | async-done | bytes 262160 | tf_op jit(solution)/shard_map/reduce_scatter | solution.py:92
  101.1 1.7 %convert_add_fusion = f32[128,4,128]{0,2,1:T(8,128)} fusion(f32[128,4,128]{0,2,1:T(8,128)} %reduce-scatter.9.cloned.1.call-done, bf16[128,4,128]{0,2,1:T(8,128)(2,1)S(1)} %collective-permute-done.3), kind=kLoop, calls=%fused_computation.52 | loop fusion | flops 131072 | bytes 655360 | tf_op jit(solution)/shard_map/add | solution.py:96
  102.9 2.8 %collective-permute-start.2 = (bf16[128,4,128]{0,2,1:T(8,128)(2,1)S(1)}, bf16[128,4,128]{0,2,1:T(8,128)(2,1)S(1)}, u32[]{:S(2)}, u32[]{:S(2)}) collective-permute-start(bf16[128,4,128]{0,2,1:T(8,128)(2,1)S(1)} %slice.23), channel_id=1, source_target_pairs={{0,14},{2,0},{4,2},{6,4},{8,6},{10,8},{12,10},{14,12},{1,15},{3,1}... | collective-permute-start | bytes 393224 | tf_op jit(solution)/shard_map/ppermute | solution.py:13
  105.7 2.5 %collective-permute-done.2 = bf16[128,4,128]{0,2,1:T(8,128)(2,1)S(1)} collective-permute-done((bf16[128,4,128]{0,2,1:T(8,128)(2,1)S(1)}, bf16[128,4,128]{0,2,1:T(8,128)(2,1)S(1)}, u32[]{:S(2)}, u32[]{:S(2)}) %collective-permute-start.2) | collective-permute-done | bytes 131104 | tf_op jit(solution)/shard_map/ppermute | solution.py:13
  108.2 9.8 %reduce-scatter.5.cloned.1.call-done = f32[128,4,128]{0,2,1:T(8,128)} async-done(((f32[256,4,128]{0,2,1:T(8,128)}), f32[128,4,128]{0,2,1:T(8,128)}) %reduce-scatter.5.cloned.1.call-update) | async-done | bytes 262160 | tf_op jit(solution)/shard_map/reduce_scatter | solution.py:91
  118.0 1.7 %convert_add_fusion.1 = f32[128,4,128]{0,2,1:T(8,128)} fusion(f32[128,4,128]{0,2,1:T(8,128)} %reduce-scatter.5.cloned.1.call-done, bf16[128,4,128]{0,2,1:T(8,128)(2,1)S(1)} %collective-permute-done.2), kind=kLoop, calls=%fused_computation.53 | loop fusion | flops 131072 | bytes 655360 | tf_op jit(solution)/shard_map/add | solution.py:95
  121.3 10.6 %reduce-scatter.11.cloned.1.call-done = f32[128,2,128]{0,2,1:T(8,128)} async-done(((f32[128,4,128]{0,2,1:T(8,128)}), f32[128,2,128]{0,2,1:T(8,128)}) %reduce-scatter.11.cloned.1.call-update) | async-done | bytes 131088 | tf_op jit(solution)/shard_map/reduce_scatter | solution.py:96
  131.9 1.7 %copy.32 = f32[128,256]{1,0:T(8,128)} copy(f32[128,256]{0,1:T(8,128)} %bitcast.75) | data formatting | bytes 262144 | tf_op jit(solution)/shard_map/reshape | solution.py:98
  133.6 12.2 %reduce-scatter.7.cloned.1.call-done = f32[128,2,128]{0,2,1:T(8,128)} async-done(((f32[128,4,128]{0,2,1:T(8,128)}), f32[128,2,128]{0,2,1:T(8,128)}) %reduce-scatter.7.cloned.1.call-update) | async-done | bytes 131088 | tf_op jit(solution)/shard_map/reduce_scatter | solution.py:95
  145.8 1.7 %copy.31 = f32[128,256]{1,0:T(8,128)} copy(f32[128,256]{0,1:T(8,128)} %bitcast.76) | data formatting | bytes 262144 | tf_op jit(solution)/shard_map/reshape | solution.py:98
  (62 shorter events, 16.4 us)
Async XLA Ops:
  7.2 1.6 %copy-start.4 = (bf16[128,512]{1,0:T(8,128)(2,1)S(1)}, bf16[128,512]{1,0:T(8,128)(2,1)}, u32[]{:S(2)}) copy-start(bf16[128,512]{1,0:T(8,128)(2,1)} %param.11) | copy-start | bytes 393220
  7.2 93.9 %reduce-scatter.9.cloned.1.call-start = ((), (), s32[]{:S(2)}) async-start(), calls=%async_computation.6 | async-start | bytes 786432 | tf_op jit(solution)/shard_map/reduce_scatter | solution.py:92
  7.2 4.4 %copy-start.5 = (s32[16]{0:T(128)S(1)}, s32[16]{0:T(128)}, u32[]{:S(2)}) copy-start(s32[16]{0:T(128)} %param.12) | copy-start | bytes 196
  7.2 6.6 %copy-start.6 = (s32[16,3]{0,1:T(4,128)S(1)}, s32[16,3]{0,1:T(4,128)}, u32[]{:S(2)}) copy-start(s32[16,3]{0,1:T(4,128)} %param.13) | copy-start | bytes 580
  8.3 17.6 %copy-start.1 = (bf16[128,2048]{1,0:T(8,128)(2,1)S(1)}, bf16[128,2048]{1,0:T(8,128)(2,1)}, u32[]{:S(2)}) copy-start(bf16[128,2048]{1,0:T(8,128)(2,1)} %param.8) | copy-start | bytes 1572868
  8.3 19.6 %collective-permute-start = (bf16[128,512]{0,1:T(8,128)(2,1)S(1)}, bf16[128,512]{0,1:T(8,128)(2,1)S(1)}, u32[]{:S(2)}, u32[]{:S(2)}) collective-permute-start(bf16[128,512]{0,1:T(8,128)(2,1)S(1)} %copy.17), channel_id=1, source_target_pairs={{0,2},{2,4},{4,6},{6,8},{8,10},{10,12},{12,14},{14,0},{1,3},{3,5},... | collective-permute-start | bytes 393224 | tf_op jit(solution)/shard_map/ppermute | solution.py:13
  8.9 19.3 %collective-permute-start.1 = (bf16[128,512]{0,1:T(8,128)(2,1)S(1)}, bf16[128,512]{0,1:T(8,128)(2,1)S(1)}, u32[]{:S(2)}, u32[]{:S(2)}) collective-permute-start(bf16[128,512]{0,1:T(8,128)(2,1)S(1)} %copy.20), channel_id=1, source_target_pairs={{0,2},{2,4},{4,6},{6,8},{8,10},{10,12},{12,14},{14,0},{1,3},{3,5},... | collective-permute-start | bytes 393224 | tf_op jit(solution)/shard_map/ppermute | solution.py:13
  25.9 1.0 copy-start.2
  84.1 2.0 %copy-start = (f32[384,4,128]{0,2,1:T(8,128)S(1)}, f32[384,4,128]{0,2,1:T(8,128)}, u32[]{:S(2)}) copy-start(f32[384,4,128]{0,2,1:T(8,128)} %get-tuple-element.53) | copy-start | bytes 2359300
  86.1 31.9 %reduce-scatter.5.cloned.1.call-start = ((), (), s32[]{:S(2)}) async-start(), calls=%async_computation.4 | async-start | bytes 786432 | tf_op jit(solution)/shard_map/reduce_scatter | solution.py:91
  87.1 44.9 %reduce-scatter.11.cloned.1.call-start = ((), (), s32[]{:S(2)}) async-start(), calls=%async_computation.7 | async-start | bytes 393216 | tf_op jit(solution)/shard_map/reduce_scatter | solution.py:96
  88.1 2.6 %collective-permute-start.3 = (bf16[128,4,128]{0,2,1:T(8,128)(2,1)S(1)}, bf16[128,4,128]{0,2,1:T(8,128)(2,1)S(1)}, u32[]{:S(2)}, u32[]{:S(2)}) collective-permute-start(bf16[128,4,128]{0,2,1:T(8,128)(2,1)S(1)} %slice.22), channel_id=1, source_target_pairs={{0,14},{2,0},{4,2},{6,4},{8,6},{10,8},{12,10},{14,12},{1,15},{3,1}... | collective-permute-start | bytes 393224 | tf_op jit(solution)/shard_map/ppermute | solution.py:13
  102.8 43.0 %reduce-scatter.7.cloned.1.call-start = ((), (), s32[]{:S(2)}) async-start(), calls=%async_computation.5 | async-start | bytes 393216 | tf_op jit(solution)/shard_map/reduce_scatter | solution.py:95
  102.9 16.8 %copy-start.3 = (bf16[4,128,4,128]{3,1,2,0:T(8,128)(2,1)S(1)}, bf16[4,128,4,128]{3,1,2,0:T(8,128)(2,1)}, u32[]{:S(2)}) copy-start(bf16[4,128,4,128]{3,1,2,0:T(8,128)(2,1)} %get-tuple-element.52) | copy-start | bytes 1572868
  102.9 5.3 %collective-permute-start.2 = (bf16[128,4,128]{0,2,1:T(8,128)(2,1)S(1)}, bf16[128,4,128]{0,2,1:T(8,128)(2,1)S(1)}, u32[]{:S(2)}, u32[]{:S(2)}) collective-permute-start(bf16[128,4,128]{0,2,1:T(8,128)(2,1)S(1)} %slice.23), channel_id=1, source_target_pairs={{0,14},{2,0},{4,2},{6,4},{8,6},{10,8},{12,10},{14,12},{1,15},{3,1}... | collective-permute-start | bytes 393224 | tf_op jit(solution)/shard_map/ppermute | solution.py:13
Sparse Core Ops, SparseCore 0:
  86.3 14.7 reduce-scatter.8
  103.4 14.5 reduce-scatter.4
  120.2 11.6 reduce-scatter.10
  134.1 11.6 reduce-scatter.6
where the time goes:
time: 155 us; the launch traced here: 154 us
  matrix products  53.8 us (35%)
  waiting for transfers between devices  48.2 us (31%)
  between operations  14.6 us (9%)
  local copies, waits for them, and re-layouts  13.1 us (8%)
  blocking collectives  11.8 us (8%)
  starting transfers between devices  6.28 us (4%)
  other arithmetic  6.18 us (4%)
    dot_general x4, matrix products, head_group(): jnp.einsum('jrw,rjd->wjd', score_grads, query_block, preferred_element_ty...  18.5 us
    dot_general x4, matrix products, head_group(): jnp.einsum('jrw,wjd->rjd', score_grads, key_window, preferred_element_typ...  13 us
    dot_general x4, matrix products, head_group(): jnp.einsum('jrw,rjd->wjd', soft_low, grad_block, preferred_element_type=j...  12.4 us
    reduce_scatter x1, waiting for transfers between devices, body(): lax.psum_scatter(own_keys + back_keys, 'dp', scatter_dimension=1, tiled=T...  12.2 us
    reduce_scatter x1, waiting for transfers between devices, body(): lax.psum_scatter(own_values + back_values, 'dp', scatter_dimension=1, til...  10.6 us
    reduce_scatter x1, waiting for transfers between devices, body(): lax.psum_scatter(value_sum[:group_span], 'inner', scatter_dimension=0, ti...  10.4 us
    reduce_scatter x1, waiting for transfers between devices, body(): lax.psum_scatter(key_sum[:group_span], 'inner', scatter_dimension=0, tile...  9.78 us
    all_gather x1, blocking collectives, body(): lax.all_gather(key_rows, 'inner', axis=0, tiled=True)  6.14 us
  transfers between devices with their start and end apart: 8, of which 6 were waited for; matrix products, arithmetic and copies ran while one was open for 8% of the time, Pallas kernels for 0%

commit v1 on v0

v1 whole, which is shorter than its diff:
```python
import functools
import math

import jax
import jax.numpy as jnp
from jax import lax
from jax.experimental import pallas as pl
from jax.experimental.pallas import tpu as pltpu
from jax.sharding import PartitionSpec as P

HD = 128
HIDDEN = -1e30
MESH = pl.DeviceIdType.MESH


def kernel(
    sizes,
    q_hbm,
    g_hbm,
    k_hbm,
    v_hbm,
    order,
    flags,
    qg_out,
    kg_out,
    vg_out,
    q,
    g,
    kw,
    vw,
    acc,
    grad_out,
    grad_in,
    half_out,
    half_in,
    local_sem,
    kv_send,
    kv_recv,
    grad_send,
    grad_recv,
    half_send,
    half_recv,
):
    n_dp, n_outer, n_inner, heads, groups = sizes
    rows = q.shape[0]
    slots = n_inner + 1
    mine = heads // n_dp
    dp, outer, inner = (lax.axis_index(name) for name in ("dp", "outer", "inner"))
    lower = lax.rem(outer + n_outer - 1, n_outer)
    upper = lax.rem(outer + 1, n_outer)

    def owner(slot):
        return {"outer": lower} if slot == n_inner else {"inner": lax.rem(inner + slot, n_inner)}

    def reader(slot):
        if slot == n_inner:
            return {"outer": upper}
        return {"inner": lax.rem(inner + n_inner - slot, n_inner)}

    def columns(head):
        return pl.ds(pl.multiple_of(head * HD, HD), HD)

    step_heads = [lax.rem(mine * (dp + 1) + k, heads) for k in range(heads)]

    local = [
        pltpu.make_async_copy(src, dst, local_sem.at[i])
        for i, (src, dst) in enumerate(
            ((k_hbm, kw.at[pl.ds(0, rows)]), (q_hbm, q), (v_hbm, vw.at[pl.ds(0, rows)]), (g_hbm, g))
        )
    ]
    for copy in local:
        copy.start()

    barrier = pltpu.get_barrier_semaphore()
    near = [{"inner": lax.rem(inner + i, n_inner)} for i in range(1, n_inner)]
    near += [{"dp": lax.rem(dp + i, n_dp)} for i in range(1, n_dp)]
    near += [{"outer": lower}, {"outer": upper}]
    for device in near:
        pl.semaphore_signal(barrier, inc=1, device_id=device, device_id_type=MESH)
    pl.semaphore_wait(barrier, len(near))

    arrivals = []
    for k in range(heads):
        cols = columns(step_heads[k])
        for slot in range(1, slots):
            for which, (src, dst) in enumerate(((k_hbm, kw), (v_hbm, vw))):
                copy = pltpu.make_async_remote_copy(
                    src_ref=src.at[:, cols],
                    dst_ref=dst.at[pl.ds(slot * rows, rows), cols],
                    send_sem=kv_send.at[k, slot - 1, which],
                    recv_sem=kv_recv.at[k, slot - 1, which],
                    device_id=reader(slot),
                    device_id_type=MESH,
                )
                copy.start()
                arrivals.append((k, copy))

    shard = outer * n_inner + inner
    own_block = order[shard]
    bias = []
    for slot in range(1, slots):
        if slot == n_inner:
            place, block = n_inner, order[lower * n_inner + inner]
        else:
            place = lax.rem(inner + slot, n_inner)
            block = order[outer * n_inner + place]
        seen = (flags[shard, place] == 1) & (block < own_block)
        bias.append(jnp.where(seen, 0.0, HIDDEN).astype(jnp.float32))

    wide = groups * rows
    key_at = lax.broadcasted_iota(jnp.int32, (rows, wide), 0)
    query_at = lax.rem(lax.broadcasted_iota(jnp.int32, (rows, wide), 1), rows)
    causal = key_at <= query_at
    scale = 1.0 / math.sqrt(HD)
    to_exp2 = scale * math.log2(math.e)

    def nt(a, b):
        return lax.dot_general(a, b, (((1,), (1,)), ((), ())), preferred_element_type=jnp.float32)

    def nn(a, b):
        return jnp.dot(a, b, preferred_element_type=jnp.float32)

    grads = []
    halves = []

    def settle(k):
        for slot in range(1, slots):
            grads[k * (slots - 1) + slot - 1].wait_recv()
        total = acc[k]
        for slot in range(1, slots):
            total += grad_in[k, slot - 1].astype(jnp.float32)
        if k < heads - mine:
            half_out[k] = total.astype(jnp.bfloat16)
            copy = pltpu.make_async_remote_copy(
                src_ref=half_out.at[k],
                dst_ref=half_in.at[k],
                send_sem=half_send.at[k],
                recv_sem=half_recv.at[k],
                device_id={"dp": lax.rem(dp + 1 + k // mine, n_dp)},
                device_id_type=MESH,
            )
            copy.start()
            halves.append(copy)
        else:
            at = k - (heads - mine)
            for d in range(n_dp - 1):
                halves[d * mine + at].wait_recv()
                total += half_in[d * mine + at].astype(jnp.float32)
            kg_out[:, at * HD : (at + 1) * HD] = total[0]
            vg_out[:, at * HD : (at + 1) * HD] = total[1]

    for copy in local:
        copy.wait()
    for k in range(heads):
        head = step_heads[k]
        cols = columns(head)
        group_cols = [columns(n * heads + head) for n in range(groups)]
        q_all = jnp.concatenate([q[:, c] for c in group_cols], 0)
        g_all = jnp.concatenate([g[:, c] for c in group_cols], 0)
        for step, copy in arrivals:
            if step == k:
                copy.wait_recv()
        keys = kw[:, cols]
        values = vw[:, cols]
        scores = nt(keys, q_all)
        weight_grads = nt(values, g_all)
        parts = [scores[c * rows : (c + 1) * rows] for c in range(slots)]
        parts[0] = jnp.where(causal, parts[0], HIDDEN)
        tops = [jnp.max(part, 0, keepdims=True) for part in parts]
        top = tops[0]
        for c in range(1, slots):
            top = jnp.maximum(top, tops[c] + bias[c - 1])
        exps = [
            jnp.exp2((part - (top if c == 0 else top - bias[c - 1])) * to_exp2)
            for c, part in enumerate(parts)
        ]
        weights = jnp.concatenate(exps, 0)
        soft = weights * (1.0 / jnp.sum(weights, 0, keepdims=True))
        delta = jnp.sum(soft * weight_grads, 0, keepdims=True)
        score_grads = (soft * (weight_grads - delta) * scale).astype(jnp.bfloat16)
        soft_low = soft.astype(jnp.bfloat16)
        key_part = nn(score_grads, q_all)
        value_part = nn(soft_low, g_all)
        acc[k, 0] = key_part[:rows]
        acc[k, 1] = value_part[:rows]
        for slot in range(1, slots):
            grad_out[k, slot - 1, 0] = key_part[slot * rows : (slot + 1) * rows].astype(jnp.bfloat16)
            grad_out[k, slot - 1, 1] = value_part[slot * rows : (slot + 1) * rows].astype(jnp.bfloat16)
            copy = pltpu.make_async_remote_copy(
                src_ref=grad_out.at[k, slot - 1],
                dst_ref=grad_in.at[k, slot - 1],
                send_sem=grad_send.at[k, slot - 1],
                recv_sem=grad_recv.at[k, slot - 1],
                device_id=owner(slot),
                device_id_type=MESH,
            )
            copy.start()
            grads.append(copy)
        query_part = nn(keys.T, score_grads)
        for n in range(groups):
            qg_out[:, group_cols[n]] = query_part[:, n * rows : (n + 1) * rows].T.astype(jnp.bfloat16)
        if k >= 2:
            settle(k - 2)
    for k in range(max(heads - 2, 0), heads):
        settle(k)
    for _, copy in arrivals:
        copy.wait_send()
    for copy in grads + halves:
        copy.wait_send()


def solution(mesh):
    n_dp, n_outer, n_inner = (mesh.shape[name] for name in ("dp", "outer", "inner"))

    def body(queries, out_grad, key_rows, value_rows, block_order, block_flags):
        rows, width = queries.shape
        heads = key_rows.shape[1] // HD
        groups = width // (heads * HD)
        mine = heads // n_dp
        others = n_inner
        bf16, f32 = jnp.bfloat16, jnp.float32
        window = (n_inner + 1) * rows
        any_space = pl.BlockSpec(memory_space=pl.ANY)
        smem = pl.BlockSpec(memory_space=pltpu.SMEM)
        vmem = pl.BlockSpec(memory_space=pltpu.VMEM)
        dma = pltpu.SemaphoreType.DMA
        return pl.pallas_call(
            functools.partial(kernel, (n_dp, n_outer, n_inner, heads, groups)),
            out_shape=(
                jax.ShapeDtypeStruct((rows, width), bf16),
                jax.ShapeDtypeStruct((rows, mine * HD), f32),
                jax.ShapeDtypeStruct((rows, mine * HD), f32),
            ),
            in_specs=[any_space] * 4 + [smem] * 2,
            out_specs=(vmem, vmem, vmem),
            scratch_shapes=[
                pltpu.VMEM((rows, width), bf16),
                pltpu.VMEM((rows, width), bf16),
                pltpu.VMEM((window, heads * HD), bf16),
                pltpu.VMEM((window, heads * HD), bf16),
                pltpu.VMEM((heads, 2, rows, HD), f32),
                pltpu.VMEM((heads, others, 2, rows, HD), bf16),
                pltpu.VMEM((heads, others, 2, rows, HD), bf16),
                pltpu.VMEM((heads - mine, 2, rows, HD), bf16),
                pltpu.VMEM((heads - mine, 2, rows, HD), bf16),
                dma((4,)),
                dma((heads, others, 2)),
                dma((heads, others, 2)),
                dma((heads, others)),
                dma((heads, others)),
                dma((heads - mine,)),
                dma((heads - mine,)),
            ],
            compiler_params=pltpu.CompilerParams(
                collective_id=0, has_side_effects=True, vmem_limit_bytes=40 * 1024 * 1024
            ),
        )(queries, out_grad, key_rows, value_rows, block_order, block_flags)

    spread = P(("outer", "inner"), "dp")
    return jax.shard_map(
        body,
        mesh=mesh,
        in_specs=(spread, spread, P(("outer", "inner"), None), P(("outer", "inner"), None), P(), P()),
        out_specs=(spread, spread, spread),
        check_vma=False,
    )
```

time: 155 us -> 28.3 us (0.18)
  matrix products: 53.8 us -> 0 us
  waiting for transfers between devices: 48.2 us -> 0 us
  Pallas kernels: 0 us -> 20.6 us
  between operations: 14.6 us -> 0.65 us
  blocking collectives: 11.8 us -> 0 us
  local copies, waits for them, and re-layouts: 13.1 us -> 6.76 us
  starting transfers between devices: 6.28 us -> 0 us
  other arithmetic: 6.18 us -> 0 us
    dot_general x20 -> x0, matrix products: 53.8 us -> none  [the longest x4 18.5 us: head_group(): jnp.einsum('jrw,rjd->wjd', score_grads, query_block, preferred_element_ty...]
    reduce_scatter x4 -> x0, waiting for transfers between devices: 43.1 us -> none  [the longest x1 12.2 us: body(): lax.psum_scatter(own_keys + back_keys, 'dp', scatter_dimension=1, tiled=T...]
    pallas_call x0 -> x1, Pallas kernels: none -> 20.6 us  [body(): pl.pallas_call(functools.partial(kernel, (n_dp, n_outer, n_inner, heads,...]
    all_gather x2 -> x0, blocking collectives: 11.8 us -> none  [the longest x1 6.14 us: body(): lax.all_gather(key_rows, 'inner', axis=0, tiled=True)]
    ppermute x4 -> x0, starting transfers between devices: 6.12 us -> none  [passed_along(): lax.ppermute(x, axis, [(i, (i + by) % devices) for i in range(devices)])]
    ppermute x4 -> x0, waiting for transfers between devices: 5.04 us -> none  [passed_along(): lax.ppermute(x, axis, [(i, (i + by) % devices) for i in range(devices)])]
    reshape x3 -> x0, local copies, waits for them, and re-layouts: 4.5 us -> none  [the longest x1 1.66 us: body(): value_grad.reshape(row_count, -1)]
    slice x4 -> x0, local copies, waits for them, and re-layouts: 3.78 us -> none  [the longest x1 1.96 us: body(): value_sum[:group_span]]
  transfers between devices with their start and end apart: 8 -> 0, of which waited for: 6 -> 0; matrix products, arithmetic and copies ran while one was open for 8% -> 0% of each run, Pallas kernels for 0% -> 0%
where the time goes in v1:
time: 28.3 us; the launch traced here: 28 us
  Pallas kernels  20.6 us (73%)
  local copies, waits for them, and re-layouts  6.76 us (24%)
  between operations  0.65 us (2%)
    pallas_call x1, Pallas kernels, body(): pl.pallas_call(functools.partial(kernel, (n_dp, n_outer, n_inner, heads,...  20.6 us
    unnamed x14, local copies, waits for them, and re-layouts  6.76 us

profile of v1, /device:TPU:0, one launch (start us, length us, event | category | flops | bytes accessed | tf_op | source)
XLA Modules:
  0.0 28.0 jit_solution(4331099101205444499)
XLA Ops:
  0.6 0.0 copy-start.4
  0.6 0.8 %copy.9.flags = s32[16,3]{1,0:T(8,128)S(1)} copy(s32[16,3]{0,1:T(4,128)} %param.11) | data formatting | bytes 384 | tf_op args[5]
  1.4 0.0 copy-done.4
  1.4 0.0 copy-start
  1.4 1.0 %copy-done = bf16[128,2048]{1,0:T(8,128)(2,1)S(1)} copy-done((bf16[128,2048]{1,0:T(8,128)(2,1)S(1)}, bf16[128,2048]{1,0:T(8,128)(2,1)}, u32[]{:S(2)}) %copy-start) | copy-done | bytes 524312
  2.5 0.0 copy-start.1
  2.5 1.0 %copy-done.1 = bf16[128,2048]{1,0:T(8,128)(2,1)S(1)} copy-done((bf16[128,2048]{1,0:T(8,128)(2,1)S(1)}, bf16[128,2048]{1,0:T(8,128)(2,1)}, u32[]{:S(2)}) %copy-start.1) | copy-done | bytes 524312
  3.5 0.0 copy-start.2
  3.5 0.9 %copy-done.2 = bf16[128,512]{1,0:T(8,128)(2,1)S(1)} copy-done((bf16[128,512]{1,0:T(8,128)(2,1)S(1)}, bf16[128,512]{1,0:T(8,128)(2,1)}, u32[]{:S(2)}) %copy-start.2) | copy-done | bytes 131096
  4.4 0.0 copy-start.3
  4.4 0.9 %copy-done.3 = bf16[128,512]{1,0:T(8,128)(2,1)S(1)} copy-done((bf16[128,512]{1,0:T(8,128)(2,1)S(1)}, bf16[128,512]{1,0:T(8,128)(2,1)}, u32[]{:S(2)}) %copy-start.3) | copy-done | bytes 131096
  5.3 20.6 %shard_map.85 = (bf16[128,2048]{1,0:T(8,128)(2,1)S(1)}, f32[128,256]{1,0:T(8,128)S(1)}, f32[128,256]{1,0:T(8,128)S(1)}) custom-call(bf16[128,2048]{1,0:T(8,128)(2,1)S(1)} %copy-done, bf16[128,2048]{1,0:T(8,128)(2,1)S(1)} %copy-done.1, bf16[128,512]{1,0:T(8,128)(2,1)S(1)} %copy-done.2, bf16[128,512]{1,0:T(8,128)(2,1)S(1)} %copy-done.3, s32[16]{0:T(128)S(1)} %copy-done.4, ...), custom_call_target="tpu_custom_call" | custom-call | tf_op jit(solution)/shard_map/pallas_call | solution.py:227
  25.9 0.8 %copy.13 = bf16[128,2048]{1,0:T(8,128)(2,1)} copy(bf16[128,2048]{1,0:T(8,128)(2,1)S(1)} %get-tuple-element.6) | data formatting | bytes 1048576
  26.7 0.7 %copy.14 = f32[128,256]{1,0:T(8,128)} copy(f32[128,256]{1,0:T(8,128)S(1)} %get-tuple-element.7) | data formatting | bytes 262144
  27.3 0.7 %copy.15 = f32[128,256]{1,0:T(8,128)} copy(f32[128,256]{1,0:T(8,128)S(1)} %get-tuple-element.8) | data formatting | bytes 262144
Async XLA Ops:
  0.6 0.8 %copy-start.4 = (s32[16]{0:T(128)S(1)}, s32[16]{0:T(128)}, u32[]{:S(2)}) copy-start(s32[16]{0:T(128)} %order.1) | copy-start | bytes 196
  1.4 1.0 %copy-start = (bf16[128,2048]{1,0:T(8,128)(2,1)S(1)}, bf16[128,2048]{1,0:T(8,128)(2,1)}, u32[]{:S(2)}) copy-start(bf16[128,2048]{1,0:T(8,128)(2,1)} %q_hbm.1) | copy-start | bytes 1572868
  2.5 1.0 %copy-start.1 = (bf16[128,2048]{1,0:T(8,128)(2,1)S(1)}, bf16[128,2048]{1,0:T(8,128)(2,1)}, u32[]{:S(2)}) copy-start(bf16[128,2048]{1,0:T(8,128)(2,1)} %g_hbm.1) | copy-start | bytes 1572868
  3.5 0.9 %copy-start.2 = (bf16[128,512]{1,0:T(8,128)(2,1)S(1)}, bf16[128,512]{1,0:T(8,128)(2,1)}, u32[]{:S(2)}) copy-start(bf16[128,512]{1,0:T(8,128)(2,1)} %k_hbm.1) | copy-start | bytes 393220
  4.4 0.9 %copy-start.3 = (bf16[128,512]{1,0:T(8,128)(2,1)S(1)}, bf16[128,512]{1,0:T(8,128)(2,1)}, u32[]{:S(2)}) copy-start(bf16[128,512]{1,0:T(8,128)(2,1)} %v_hbm.1) | copy-start | bytes 393220

commit v2 on v1

--- a/solution.py
+++ b/solution.py
@@ -40,6 +40,9 @@
     grad_recv,
     half_send,
     half_recv,
+    cross_in,
+    cross_recv,
+    pass_send,
 ):
     n_dp, n_outer, n_inner, heads, groups = sizes
     rows = q.shape[0]
@@ -79,21 +82,54 @@
         pl.semaphore_signal(barrier, inc=1, device_id=device, device_id_type=MESH)
     pl.semaphore_wait(barrier, len(near))
 
-    arrivals = []
+    def window(ref, slot, k):
+        return ref.at[pl.ds(slot * rows, rows), columns(step_heads[k])]
+
+    def arriving(src, dst, k, slot, which, send_sem, device, at):
+        return pltpu.make_async_remote_copy(
+            src_ref=src,
+            dst_ref=window(dst, slot, k),
+            send_sem=send_sem,
+            recv_sem=kv_recv.at[at, slot - 1, which],
+            device_id=device,
+            device_id_type=MESH,
+        )
+
+    pairs = ((k_hbm, kw), (v_hbm, vw))
+    arrivals = {}
+    sent = []
     for k in range(heads):
-        cols = columns(step_heads[k])
         for slot in range(1, slots):
-            for which, (src, dst) in enumerate(((k_hbm, kw), (v_hbm, vw))):
-                copy = pltpu.make_async_remote_copy(
-                    src_ref=src.at[:, cols],
-                    dst_ref=dst.at[pl.ds(slot * rows, rows), cols],
-                    send_sem=kv_send.at[k, slot - 1, which],
-                    recv_sem=kv_recv.at[k, slot - 1, which],
-                    device_id=reader(slot),
-                    device_id_type=MESH,
+            direct = slot == n_inner or k < mine
+            for which, (src, dst) in enumerate(pairs):
+                block = src.at[:, columns(step_heads[k])] if direct else window(dst, slot, k)
+                copy = arriving(
+                    block, dst, k, slot, which, kv_send.at[k, slot - 1, which], reader(slot), k
                 )
-                copy.start()
-                arrivals.append((k, copy))
+                if direct:
+                    copy.start()
+                    sent.append(copy)
+                arrivals[k, slot, which] = copy
+
+    def arrive(k):
+        for slot in range(1, slots):
+            for which, (_, dst) in enumerate(pairs):
+                arrivals[k, slot, which].wait_recv()
+                if slot == n_inner or k >= mine:
+                    continue
+                for d in range(1, n_dp):
+                    copy = arriving(
+                        window(dst, slot, k),
+                        dst,
+                        k,
+                        slot,
+                        which,
+                        pass_send.at[d - 1, k, slot - 1, which],
+                        {"dp": lax.rem(dp + d, n_dp)},
+                        mine * (n_dp - d) + k,
+                    )
+                    copy.start()
+                    sent.append(copy)
 
     shard = outer * n_inner + inner
     own_block = order[shard]
@@ -104,7 +140,7 @@
         else:
             place = lax.rem(inner + slot, n_inner)
             block = order[outer * n_inner + place]
-        seen = (flags[shard, place] == 1) & (block < own_block)
+        seen = (flags[place, shard] == 1) & (block < own_block)
         bias.append(jnp.where(seen, 0.0, HIDDEN).astype(jnp.float32))
 
     wide = groups * rows
@@ -120,14 +156,20 @@
     def nn(a, b):
         return jnp.dot(a, b, preferred_element_type=jnp.float32)
 
-    grads = []
+    grads = {}
+    crossing = {}
     halves = []
 
+    def crosses(k, slot):
+        return slot < n_inner and k < heads - mine and k % mine < mine // 2
+
+
     def settle(k):
-        for slot in range(1, slots):
-            grads[k * (slots - 1) + slot - 1].wait_recv()
         total = acc[k]
         for slot in range(1, slots):
+            if crosses(k, slot):
+                continue
+            grads[k, slot].wait_recv()
             total += grad_in[k, slot - 1].astype(jnp.float32)
         if k < heads - mine:
             half_out[k] = total.astype(jnp.bfloat16)
@@ -157,9 +199,7 @@
         group_cols = [columns(n * heads + head) for n in range(groups)]
         q_all = jnp.concatenate([q[:, c] for c in group_cols], 0)
         g_all = jnp.concatenate([g[:, c] for c in group_cols], 0)
-        for step, copy in arrivals:
-            if step == k:
-                copy.wait_recv()
+        arrive(k)
         keys = kw[:, cols]
         values = vw[:, cols]
         scores = nt(keys, q_all)
@@ -184,18 +224,36 @@
         acc[k, 0] = key_part[:rows]
         acc[k, 1] = value_part[:rows]
         for slot in range(1, slots):
-            grad_out[k, slot - 1, 0] = key_part[slot * rows : (slot + 1) * rows].astype(jnp.bfloat16)
-            grad_out[k, slot - 1, 1] = value_part[slot * rows : (slot + 1) * rows].astype(jnp.bfloat16)
-            copy = pltpu.make_async_remote_copy(
-                src_ref=grad_out.at[k, slot - 1],
-                dst_ref=grad_in.at[k, slot - 1],
-                send_sem=grad_send.at[k, slot - 1],
-                recv_sem=grad_recv.at[k, slot - 1],
-                device_id=owner(slot),
-                device_id_type=MESH,
-            )
+            terms = [x[slot * rows : (slot + 1) * rows] for x in (key_part, value_part)]
+            at = k - (heads - mine)
+            if at >= 0 and slot < n_inner and at < mine // 2:
+                for d in range(n_dp - 1):
+                    crossing[d * mine + at, slot].wait_recv()
+                    for which in range(2):
+                        terms[which] += cross_in[d * mine + at, slot - 1, which].astype(jnp.float32)
+            for which in range(2):
+                grad_out[k, slot - 1, which] = terms[which].astype(jnp.bfloat16)
+            if crosses(k, slot):
+                copy = pltpu.make_async_remote_copy(
+                    src_ref=grad_out.at[k, slot - 1],
+                    dst_ref=cross_in.at[k, slot - 1],
+                    send_sem=grad_send.at[k, slot - 1],
+                    recv_sem=cross_recv.at[k, slot - 1],
+                    device_id={"dp": lax.rem(dp + 1 + k // mine, n_dp)},
+                    device_id_type=MESH,
+                )
+                crossing[k, slot] = copy
+            else:
+                copy = pltpu.make_async_remote_copy(
+                    src_ref=grad_out.at[k, slot - 1],
+                    dst_ref=grad_in.at[k, slot - 1],
+                    send_sem=grad_send.at[k, slot - 1],
+                    recv_sem=grad_recv.at[k, slot - 1],
+                    device_id=owner(slot),
+                    device_id_type=MESH,
+                )
+                grads[k, slot] = copy
             copy.start()
-            grads.append(copy)
         query_part = nn(keys.T, score_grads)
         for n in range(groups):
             qg_out[:, group_cols[n]] = query_part[:, n * rows : (n + 1) * rows].T.astype(jnp.bfloat16)
@@ -203,10 +261,19 @@
             settle(k - 2)
     for k in range(max(heads - 2, 0), heads):
         settle(k)
-    for _, copy in arrivals:
+    for copy in sent + list(grads.values()) + list(crossing.values()) + halves:
         copy.wait_send()
-    for copy in grads + halves:
-        copy.wait_send()
+
+
+def place(*refs):
+    *arrays, sems = refs
+    copies = [
+        pltpu.make_async_copy(arrays[i], arrays[i + 3], sems.at[i]) for i in range(3)
+    ]
+    for copy in copies:
+        copy.start()
+    for copy in copies:
+        copy.wait()
 
 
 def solution(mesh):
@@ -224,12 +291,16 @@
         smem = pl.BlockSpec(memory_space=pltpu.SMEM)
         vmem = pl.BlockSpec(memory_space=pltpu.VMEM)
         dma = pltpu.SemaphoreType.DMA
-        return pl.pallas_call(
+        operands = [
+            pltpu.with_memory_space_constraint(x, pltpu.HBM)
+            for x in (queries, out_grad, key_rows, value_rows, block_order, block_flags.T)
+        ]
+        results = pl.pallas_call(
             functools.partial(kernel, (n_dp, n_outer, n_inner, heads, groups)),
             out_shape=(
-                jax.ShapeDtypeStruct((rows, width), bf16),
-                jax.ShapeDtypeStruct((rows, mine * HD), f32),
-                jax.ShapeDtypeStruct((rows, mine * HD), f32),
+                pltpu.VMEM((rows, width), bf16),
+                pltpu.VMEM((rows, mine * HD), f32),
+                pltpu.VMEM((rows, mine * HD), f32),
             ),
             in_specs=[any_space] * 4 + [smem] * 2,
             out_specs=(vmem, vmem, vmem),
@@ -250,11 +321,21 @@
                 dma((heads, others)),
                 dma((heads - mine,)),
                 dma((heads - mine,)),
+                pltpu.VMEM((heads - mine, others, 2, rows, HD), bf16),
+                dma((heads - mine, others)),
+                dma((n_dp - 1, mine, others, 2)),
             ],
             compiler_params=pltpu.CompilerParams(
                 collective_id=0, has_side_effects=True, vmem_limit_bytes=40 * 1024 * 1024
             ),
-        )(queries, out_grad, key_rows, value_rows, block_order, block_flags)
+        )(*operands)
+        return pl.pallas_call(
+            place,
+            out_shape=tuple(pltpu.HBM(x.shape, x.dtype) for x in results),
+            in_specs=[vmem] * 3,
+            out_specs=(any_space,) * 3,
+            scratch_shapes=[dma((3,))],
+        )(*(pltpu.with_memory_space_constraint(x, pltpu.VMEM) for x in results))
 
     spread = P(("outer", "inner"), "dp")
     return jax.shard_map(

time: 28.3 us -> 20.9 us (0.74)
  local copies, waits for them, and re-layouts: 6.76 us -> 0 us
  Pallas kernels: 20.6 us -> 20.1 us
    unnamed x14 -> x0, local copies, waits for them, and re-layouts: 6.76 us -> none
    pallas_call x1, Pallas kernels: 20.6 us -> 19.2 us  [body(): pl.pallas_call(functools.partial(kernel, (n_dp, n_outer, n_inner, heads,...]
    pallas_call x0 -> x1, Pallas kernels: none -> 0.9 us  [body(): pl.pallas_call(place, out_shape=tuple((pltpu.HBM(x.shape, x.dtype) for x...]
where the time goes in v2:
time: 20.9 us; the launch traced here: 20.7 us
  Pallas kernels  20.1 us (96%)
  between operations  0.64 us (3%)
    pallas_call x1, Pallas kernels, body(): pl.pallas_call(functools.partial(kernel, (n_dp, n_outer, n_inner, heads,...  19.2 us
    pallas_call x1, Pallas kernels, body(): pl.pallas_call(place, out_shape=tuple((pltpu.HBM(x.shape, x.dtype) for x...  0.9 us

profile of v2, /device:TPU:0, one launch (start us, length us, event | category | flops | bytes accessed | tf_op | source)
XLA Modules:
  0.0 20.7 jit_solution(17890602493495032211)
XLA Ops:
  0.6 19.2 %shard_map.85 = (bf16[128,2048]{1,0:T(8,128)(2,1)S(1)}, f32[128,256]{1,0:T(8,128)S(1)}, f32[128,256]{1,0:T(8,128)S(1)}) custom-call(bf16[128,2048]{1,0:T(8,128)(2,1)} %q_hbm.1, bf16[128,2048]{1,0:T(8,128)(2,1)} %g_hbm.1, bf16[128,512]{1,0:T(8,128)(2,1)} %k_hbm.1, bf16[128,512]{1,0:T(8,128)(2,1)} %v_hbm.1, s32[16]{0:T(128)} %order.1, s32[3,16]{1,0:T(4,128)} %bitcast.1), custom_call_target="tpu_custom_call" | custom-call | tf_op jit(solution)/shard_map/pallas_call | solution.py:298
  19.8 0.9 %shard_map.86 = (bf16[128,2048]{1,0:T(8,128)(2,1)}, f32[128,256]{1,0:T(8,128)}, f32[128,256]{1,0:T(8,128)}) custom-call(bf16[128,2048]{1,0:T(8,128)(2,1)S(1)} %get-tuple-element.6.refs_0_, f32[128,256]{1,0:T(8,128)S(1)} %get-tuple-element.7.refs_1_, f32[128,256]{1,0:T(8,128)S(1)} %get-tuple-element.8.refs_2_), custom_call_target="tpu_custom_call" | custom-call | tf_op jit(solution)/shard_map/pallas_call | solution.py:332

commit v3 on v2

--- a/solution.py
+++ b/solution.py
@@ -43,6 +43,7 @@
     cross_in,
     cross_recv,
     pass_send,
+    own,
 ):
     n_dp, n_outer, n_inner, heads, groups = sizes
     rows = q.shape[0]
@@ -191,21 +192,28 @@
             kg_out[:, at * HD : (at + 1) * HD] = total[0]
             vg_out[:, at * HD : (at + 1) * HD] = total[1]
 
+    def stacked(k):
+        group_cols = [columns(n * heads + step_heads[k]) for n in range(groups)]
+        q_all = jnp.concatenate([q[:, c] for c in group_cols], 0)
+        g_all = jnp.concatenate([g[:, c] for c in group_cols], 0)
+        return group_cols, q_all, g_all
+
     for copy in local:
         copy.wait()
     for k in range(heads):
-        head = step_heads[k]
-        cols = columns(head)
-        group_cols = [columns(n * heads + head) for n in range(groups)]
-        q_all = jnp.concatenate([q[:, c] for c in group_cols], 0)
-        g_all = jnp.concatenate([g[:, c] for c in group_cols], 0)
+        cols = columns(step_heads[k])
+        _, q_all, g_all = stacked(k)
+        own[k, 0] = jnp.where(causal, nt(kw[:rows, cols], q_all), HIDDEN)
+        own[k, 1] = nt(vw[:rows, cols], g_all)
+    for k in range(heads):
+        cols = columns(step_heads[k])
+        group_cols, q_all, g_all = stacked(k)
         arrive(k)
         keys = kw[:, cols]
         values = vw[:, cols]
-        scores = nt(keys, q_all)
-        weight_grads = nt(values, g_all)
-        parts = [scores[c * rows : (c + 1) * rows] for c in range(slots)]
-        parts[0] = jnp.where(causal, parts[0], HIDDEN)
+        scores = nt(keys[rows:], q_all)
+        weight_grads = jnp.concatenate([own[k, 1], nt(values[rows:], g_all)], 0)
+        parts = [own[k, 0]] + [scores[c * rows : (c + 1) * rows] for c in range(slots - 1)]
         tops = [jnp.max(part, 0, keepdims=True) for part in parts]
         top = tops[0]
         for c in range(1, slots):
@@ -324,6 +332,7 @@
                 pltpu.VMEM((heads - mine, others, 2, rows, HD), bf16),
                 dma((heads - mine, others)),
                 dma((n_dp - 1, mine, others, 2)),
+                pltpu.VMEM((heads, 2, rows, groups * rows), f32),
             ],
             compiler_params=pltpu.CompilerParams(
                 collective_id=0, has_side_effects=True, vmem_limit_bytes=40 * 1024 * 1024

time: 20.9 us -> 20.7 us (level)
  no operation moved by 1% of the time
where the time goes in v3:
time: 20.7 us; the launch traced here: 20.5 us
  Pallas kernels  19.9 us (96%)
  between operations  0.64 us (3%)
    pallas_call x1, Pallas kernels, body(): pl.pallas_call(functools.partial(kernel, (n_dp, n_outer, n_inner, heads,...  19 us
    pallas_call x1, Pallas kernels, body(): pl.pallas_call(place, out_shape=tuple((pltpu.HBM(x.shape, x.dtype) for x...  0.9 us

profile of v3, /device:TPU:0, one launch (start us, length us, event | category | flops | bytes accessed | tf_op | source)
XLA Modules:
  0.0 20.5 jit_solution(13743797209076199052)
XLA Ops:
  0.6 19.0 %shard_map.85 = (bf16[128,2048]{1,0:T(8,128)(2,1)S(1)}, f32[128,256]{1,0:T(8,128)S(1)}, f32[128,256]{1,0:T(8,128)S(1)}) custom-call(bf16[128,2048]{1,0:T(8,128)(2,1)} %q_hbm.1, bf16[128,2048]{1,0:T(8,128)(2,1)} %g_hbm.1, bf16[128,512]{1,0:T(8,128)(2,1)} %k_hbm.1, bf16[128,512]{1,0:T(8,128)(2,1)} %v_hbm.1, s32[16]{0:T(128)} %order.1, s32[3,16]{1,0:T(4,128)} %bitcast.1), custom_call_target="tpu_custom_call" | custom-call | tf_op jit(solution)/shard_map/pallas_call | solution.py:306
  19.6 0.9 %shard_map.86 = (bf16[128,2048]{1,0:T(8,128)(2,1)}, f32[128,256]{1,0:T(8,128)}, f32[128,256]{1,0:T(8,128)}) custom-call(bf16[128,2048]{1,0:T(8,128)(2,1)S(1)} %get-tuple-element.6.refs_0_, f32[128,256]{1,0:T(8,128)S(1)} %get-tuple-element.7.refs_1_, f32[128,256]{1,0:T(8,128)S(1)} %get-tuple-element.8.refs_2_), custom_call_target="tpu_custom_call" | custom-call | tf_op jit(solution)/shard_map/pallas_call | solution.py:341
